TPU v7x, 32 devices: a whole 2x2x4 slice. The times are simulated.
32 devices in a mesh: gx: 4 (over y, core), gy: 8 (over z, x).
Axes of the slice: x: 2, y: 2, z: 4, core: 2. Of those that a mesh axis runs over, the one named last changes fastest.
Arguments:
- skip_input: bfloat16 [32, 16, 2048], P(None, 'gx', 'gy'), may hold values from -6 to 6
- w_encoder: bfloat16 [64, 864], replicated, may hold values from -0.625 to 0.625
- w_bottom: bfloat16 [128, 1728], P('gx'), may hold values from -0.3125 to 0.3125
- w_middle: bfloat16 [64, 5184], replicated, may hold values from -0.15625 to 0.15625
- w_upper: bfloat16 [32, 2592], replicated, may hold values from -0.21875 to 0.21875
- cotangent: bfloat16 [32, 16, 2048], P(None, 'gx', 'gy'), may hold values from -6 to 6
Outputs:
- features: bfloat16 [32, 16, 2048], P(None, 'gx', 'gy')
- grad_skip: bfloat16 [32, 16, 2048], P(None, 'gx', 'gy')
- grad_encoder: float32 [64, 864], replicated
- grad_bottom: float32 [128, 1728], P('gx')
- grad_middle: float32 [64, 5184], replicated
- grad_upper: float32 [32, 2592], replicated
All inputs are finite; a program needn't handle non-finite values.
Results may differ from a plain program's by a relative error of at most 0.017.
Values may be sent and summed in bfloat16 or wider, within the bound.
A program may use at most 64 MiB of HBM per device.

v0:
```python
import functools
import math

import jax
import jax.numpy as jnp
from jax import lax
from jax.experimental import pallas as pl
from jax.experimental.pallas import tpu as pltpu
from jax.sharding import PartitionSpec as P

Z = 16
MESH = pl.DeviceIdType.MESH
VMEM = pl.BlockSpec(memory_space=pltpu.VMEM)
SIDES = ((-1, -1), (-1, 0), (-1, 1), (0, -1), (0, 1), (1, -1), (1, 0), (1, 1))


def halo_kernel(rows_count, cols_count, *refs):
    sent, landed, (send_sem, recv_sem) = refs[:8], refs[8:16], refs[16:]
    row, col = lax.axis_index("gx"), lax.axis_index("gy")
    barrier = pltpu.get_barrier_semaphore()

    def place(side):
        to_row, to_col = row + side[0], col + side[1]
        inside = (to_row >= 0) & (to_row < rows_count) & (to_col >= 0) & (to_col < cols_count)
        return inside, (to_row, to_col)

    for side in SIDES:
        inside, device = place(side)

        @pl.when(inside)
        def _(device=device):
            pl.semaphore_signal(barrier, inc=1, device_id=device, device_id_type=MESH)

    near_rows = 1 + (row > 0).astype(jnp.int32) + (row < rows_count - 1).astype(jnp.int32)
    near_cols = 1 + (col > 0).astype(jnp.int32) + (col < cols_count - 1).astype(jnp.int32)
    pl.semaphore_wait(barrier, near_rows * near_cols - 1)

    def copy(number, device):
        return pltpu.make_async_remote_copy(
            src_ref=sent[number],
            dst_ref=landed[7 - number],
            send_sem=send_sem.at[number],
            recv_sem=recv_sem.at[7 - number],
            device_id=device,
            device_id_type=MESH,
        )

    for number, side in enumerate(SIDES):
        inside, device = place(side)

        @pl.when(inside)
        def _(number=number, device=device):
            copy(number, device).start()

        @pl.when(jnp.logical_not(inside))
        def _(number=number):
            landed[number][...] = jnp.zeros_like(landed[number])

    for number, side in enumerate(SIDES):
        inside, device = place(side)

        @pl.when(inside)
        def _(number=number, device=device):
            copy(number, device).wait_send()
            copy(7 - number, device).wait_recv()


def spatial_halo(cells, width, number):
    channels, rows, length = cells.shape
    strips, shapes = [], []
    for side in SIDES:
        part = cells
        if side[0] != 0:
            part = part[:, :1] if side[0] < 0 else part[:, rows - 1 :]
        if side[1] != 0:
            part = part[:, :, :width] if side[1] < 0 else part[:, :, length - width :]
        shapes.append(part.shape)
        flat = part.reshape(channels, -1)
        strips.append(jnp.pad(flat, ((0, 0), (0, -flat.shape[1] % 128))))
    landed = pl.pallas_call(
        functools.partial(halo_kernel, lax.axis_size("gx"), lax.axis_size("gy")),
        out_shape=[jax.ShapeDtypeStruct(strip.shape, strip.dtype) for strip in strips],
        in_specs=[VMEM] * 8,
        out_specs=[VMEM] * 8,
        scratch_shapes=[pltpu.SemaphoreType.DMA((8,)), pltpu.SemaphoreType.DMA((8,))],
        compiler_params=pltpu.CompilerParams(collective_id=number, has_side_effects=True),
    )(*strips)
    parts = [
        strip[:, : shape[1] * shape[2]].reshape(shape) for strip, shape in zip(landed, shapes)
    ]
    return jnp.concatenate(
        [
            jnp.concatenate(parts[0:3], axis=2),
            jnp.concatenate([parts[3], cells, parts[4]], axis=2),
            jnp.concatenate(parts[5:8], axis=2),
        ],
        axis=1,
    )


def sum_kernel(nx, ny, q, s, big, low, out_big, out_low, first, work, second, result, *sems):
    row, col = lax.axis_index("gx"), lax.axis_index("gy")
    send_one, recv_one, send_two, recv_two, send_three, recv_three, send_four, recv_four = sems
    barrier = pltpu.get_barrier_semaphore()

    def on_row(step):
        return (lax.rem(row + step + nx, nx), col)

    def on_col(step):
        return (row, lax.rem(col + step + ny, ny))

    for step in range(1, nx):
        pl.semaphore_signal(barrier, inc=1, device_id=on_row(step), device_id_type=MESH)
    for step in range(1, ny):
        pl.semaphore_signal(barrier, inc=1, device_id=on_col(step), device_id_type=MESH)
    pl.semaphore_wait(barrier, nx + ny - 2)

    def part(ref, index, width):
        return ref.at[:, pl.ds(pl.multiple_of(index * width, 128), width)]

    def copy(source, target, send, recv, step, device):
        return pltpu.make_async_remote_copy(
            src_ref=source,
            dst_ref=target,
            send_sem=send.at[step],
            recv_sem=recv.at[step],
            device_id=device,
            device_id_type=MESH,
        )

    pending = []
    for step in range(1, nx):
        device = on_row(step)
        pending.append(
            copy(part(big, device[0], q), first.at[step], send_one, recv_one, step, device)
        )
        pending[-1].start()
    width = low.shape[1]
    work[:, pl.ds(q, width)] = low[...]
    if work.shape[1] > q + width:
        rest = work.shape[1] - q - width
        work[:, pl.ds(q + width, rest)] = jnp.zeros((work.shape[0], rest), work.dtype)
    total = part(big, row, q)[...].astype(jnp.float32)
    for step in range(1, nx):
        pending[step - 1].wait_recv()
        total = total + first[step].astype(jnp.float32)
    work[:, pl.ds(0, q)] = total.astype(work.dtype)

    base = len(pending)
    for step in range(1, ny):
        device = on_col(step)
        pending.append(
            copy(part(work, device[1], s), second.at[step], send_two, recv_two, step, device)
        )
        pending[-1].start()
    total = part(work, col, s)[...].astype(jnp.float32)
    for step in range(1, ny):
        pending[base + step - 1].wait_recv()
        total = total + second[step].astype(jnp.float32)
    part(result, col, s)[...] = total.astype(result.dtype)

    for step in range(1, ny):
        device = on_col(step)
        block = part(result, col, s)
        pending.append(copy(block, block, send_three, recv_three, step, device))
        pending[-1].start()
    for step in range(1, ny):
        came = on_col(-step)
        block = part(result, came[1], s)
        copy(block, block, send_three, recv_three, step, came).wait_recv()

    block = result.at[:, pl.ds(0, q)]
    for step in range(1, nx):
        device = on_row(step)
        pending.append(copy(block, part(out_big, row, q), send_four, recv_four, step, device))
        pending[-1].start()
    part(out_big, row, q)[...] = block[...]
    out_low[...] = result[:, pl.ds(q, width)]
    for step in range(1, nx):
        came = on_row(-step)
        copy(block, part(out_big, came[0], q), send_four, recv_four, step, came).wait_recv()
    for sent in pending:
        sent.wait_send()


def folded(grad, rows):
    width = grad.shape[1] * grad.shape[0] // rows
    return jnp.concatenate(
        [grad[:, i * width : (i + 1) * width] for i in range(rows // grad.shape[0])], axis=0
    )


def unfolded(grad, shape):
    count = grad.shape[0] // shape[0]
    return jnp.concatenate(
        [grad[i * shape[0] : (i + 1) * shape[0]] for i in range(count)], axis=1
    ).astype(jnp.float32)


def round_up(value, unit):
    return -(-value // unit) * unit


def summed(grads, low_grad, number):
    nx, ny = lax.axis_size("gx"), lax.axis_size("gy")
    rows = max(grad.shape[0] for grad in grads)
    wide = [folded(grad.astype(jnp.bfloat16), rows) for grad in grads]
    low = folded(low_grad.astype(jnp.bfloat16), rows)
    count = sum(grad.shape[1] for grad in wide)
    q = round_up(round_up(count, nx) // nx, 128)
    width = round_up(low.shape[1], 128)
    s = round_up(round_up(q + width, ny) // ny, 128)
    fill = jnp.zeros((rows, nx * q - count), jnp.bfloat16)
    big = jnp.concatenate(wide + [fill], axis=1)
    low_fill = jnp.pad(low, ((0, 0), (0, width - low.shape[1])))
    out_big, out_low = pl.pallas_call(
        functools.partial(sum_kernel, nx, ny, q, s),
        out_shape=[
            jax.ShapeDtypeStruct(big.shape, big.dtype),
            jax.ShapeDtypeStruct(low_fill.shape, low_fill.dtype),
        ],
        in_specs=[VMEM] * 2,
        out_specs=[VMEM] * 2,
        scratch_shapes=[
            pltpu.VMEM((nx, rows, q), jnp.bfloat16),
            pltpu.VMEM((rows, ny * s), jnp.bfloat16),
            pltpu.VMEM((ny, rows, s), jnp.bfloat16),
            pltpu.VMEM((rows, ny * s), jnp.bfloat16),
        ]
        + [pltpu.SemaphoreType.DMA((count,)) for count in (nx, nx, ny, ny, ny, ny, nx, nx)],
        compiler_params=pltpu.CompilerParams(
            collective_id=number, has_side_effects=True, vmem_limit_bytes=32 << 20
        ),
    )(big, low_fill)
    results, start = [], 0
    for grad, piece in zip(grads, wide):
        results.append(unfolded(out_big[:, start : start + piece.shape[1]], grad.shape))
        start += piece.shape[1]
    return results, unfolded(out_low[:, : low.shape[1]], low_grad.shape)


def extended_2(cells, sides, width):
    for axis, dim in sides:
        count = lax.axis_size(axis)
        ends = count - 1
        head = lax.slice_in_dim(cells, 0, width, axis=dim)
        tail = lax.slice_in_dim(cells, cells.shape[dim] - width, cells.shape[dim], axis=dim)
        cells = jnp.concatenate(
            [
                lax.ppermute(tail, axis, [(i, (i + 1) % count) for i in range(ends)]),
                cells,
                lax.ppermute(head, axis, [((i + 1) % count, i) for i in range(ends)]),
            ],
            axis=dim,
        )
    return cells


def stack_taps(x_ref, stack, z_depth):
    channels, length = x_ref.shape
    values = x_ref[...].astype(jnp.float32)
    z_index = lax.broadcasted_iota(jnp.int32, (channels, length), 1) % z_depth
    for b in range(3):
        for c in range(3):
            moved = pltpu.roll(values, (length - b * z_depth - c + 1) % length, 1)
            if c != 1:
                moved = jnp.where(z_index != (0 if c == 0 else z_depth - 1), moved, 0.0)
            tap = 3 * b + c
            stack[tap * channels : (tap + 1) * channels, :] = moved.astype(jnp.bfloat16)
    if stack.shape[0] > 9 * channels:
        rest = stack.shape[0] - 9 * channels
        stack[9 * channels :, :] = jnp.zeros((rest, length), jnp.bfloat16)


def conv_kernel(z_depth, row_count, x_ref, w_ref, out_ref, stack):
    stack_taps(x_ref, stack, z_depth)
    length = x_ref.shape[1] // (row_count + 2)
    total = jnp.dot(w_ref[...], stack[...], preferred_element_type=jnp.float32)
    chan = out_ref.shape[0]
    out_ref[...] = sum(
        total[a * chan : (a + 1) * chan, a * length : (a + row_count) * length] for a in range(3)
    )


def grad_kernel(z_depth, row_count, x_ref, error_ref, out_ref, stack):
    stack_taps(x_ref, stack, z_depth)
    length = x_ref.shape[1] // (row_count + 2)
    for a in range(3):
        out_ref[a] = lax.dot_general(
            error_ref[...],
            stack[:, a * length : (a + row_count) * length],
            (((1,), (1,)), ((), ())),
            preferred_element_type=jnp.float32,
        )


def widened(values, length):
    padded = jnp.pad(values, ((0, 0), (0, 0), (0, length - values.shape[2])))
    return padded.reshape(values.shape[0], -1)


def local_call(kernel, extended, other, out_shape, row_count, z_depth):
    length = round_up(extended.shape[2], 128)
    flat = widened(extended, length)
    depth = round_up(9 * flat.shape[0], 128)
    return pl.pallas_call(
        functools.partial(kernel, z_depth, row_count),
        out_shape=jax.ShapeDtypeStruct(out_shape, jnp.float32),
        in_specs=[VMEM] * 2,
        out_specs=VMEM,
        scratch_shapes=[pltpu.VMEM((depth, flat.shape[1]), jnp.bfloat16)],
        compiler_params=pltpu.CompilerParams(vmem_limit_bytes=40 << 20),
    )(flat, other)


def conv_local(extended, taps, out_chan, row_count, col_count, z_depth):
    length = round_up(extended.shape[2], 128)
    weight = taps.reshape(3 * out_chan, -1)
    weight = jnp.pad(weight, ((0, 0), (0, -weight.shape[1] % 128)))
    out = local_call(
        conv_kernel, extended, weight, (out_chan, row_count * length), row_count, z_depth
    )
    out = out.reshape(out_chan, row_count, length)[:, :, : col_count * z_depth]
    return out.reshape(out_chan, -1)


def conv_forward(extended, weight, row_count, col_count, z_depth):
    out_chan = weight.shape[0]
    taps = weight.reshape(out_chan, 3, -1).transpose(1, 0, 2)
    return conv_local(extended, taps, out_chan, row_count, col_count, z_depth)


def conv_backward(extended, weight, row_count, col_count, z_depth):
    out_chan, in_chan = weight.shape[0], weight.shape[1] // 27
    taps = weight.reshape(out_chan, 27, in_chan)[:, ::-1].transpose(1, 2, 0)
    taps = taps.reshape(3, 9, in_chan, out_chan).transpose(0, 2, 1, 3)
    return conv_local(extended, taps, in_chan, row_count, col_count, z_depth)


def weight_grad(extended, error_flat, row_count, col_count, z_depth):
    in_chan, out_chan = extended.shape[0], error_flat.shape[0]
    error = widened(
        error_flat.reshape(out_chan, row_count, -1), round_up(extended.shape[2], 128)
    )
    shape = (3, out_chan, round_up(9 * in_chan, 128))
    out = local_call(grad_kernel, extended, error, shape, row_count, z_depth)
    return jnp.concatenate([out[a, :, : 9 * in_chan] for a in range(3)], axis=1)


def pool_mean(values, z_depth):
    channels, row_count, length = values.shape
    col_count = length // z_depth
    shaped = values.astype(jnp.float32).reshape(
        channels, row_count // 2, 2, col_count // 2, 2, z_depth // 2, 2
    )
    return shaped.mean(axis=(2, 4, 6)).reshape(
        channels, row_count // 2, col_count // 2 * (z_depth // 2)
    )


def block_sum(values, z_depth):
    channels, row_count, length = values.shape
    col_count = length // z_depth
    shaped = values.reshape(channels, row_count // 2, 2, col_count // 2, 2, z_depth // 2, 2)
    return shaped.sum(axis=(2, 4, 6)).reshape(
        channels, row_count // 2, col_count // 2 * (z_depth // 2)
    )


def upsample(values, z_depth):
    channels, row_count, length = values.shape
    col_count = length // z_depth
    shaped = values.reshape(channels, row_count, 1, col_count, 1, z_depth, 1)
    shaped = jnp.broadcast_to(shaped, (channels, row_count, 2, col_count, 2, z_depth, 2))
    return shaped.reshape(channels, 2 * row_count, 4 * col_count * z_depth)


def silu_slope(values):
    s_value = jax.nn.sigmoid(values)
    return s_value * (1.0 + values * (1.0 - s_value))


def per_device(skip_input, w_encoder, w_bottom, w_middle, w_upper, cotangent):
    top_chan = skip_input.shape[0]
    rows_fine = skip_input.shape[1]
    cols_fine = skip_input.shape[2] // Z
    rows_mid, cols_mid, depth_mid = (rows_fine // 2, cols_fine // 2, Z // 2)
    rows_low, cols_low, depth_low = (rows_fine // 4, cols_fine // 4, Z // 4)
    cells_fine = rows_fine * cols_fine * Z * lax.axis_size("gx") * lax.axis_size("gy")
    scale_fine = 1.0 / math.sqrt(cells_fine)
    scale_mid = 1.0 / math.sqrt(cells_fine // 8)
    scale_low = 1.0 / math.sqrt(cells_fine // 64)
    pool_top = pool_mean(skip_input, Z).astype(jnp.bfloat16)
    ext_pool = spatial_halo(pool_top, depth_mid, 0)
    pre_one = conv_forward(ext_pool, w_encoder, rows_mid, cols_mid, depth_mid)
    act_one = jax.nn.silu(pre_one).astype(jnp.bfloat16).reshape(-1, rows_mid, cols_mid * depth_mid)
    pool_mid = pool_mean(act_one, depth_mid).astype(jnp.bfloat16)
    col_ext = extended_2(pool_mid, (("gy", 2),), depth_low)
    whole_rows = lax.all_gather(col_ext, "gx", axis=1, tiled=True)
    ext_low = jnp.pad(whole_rows, ((0, 0), (1, 1), (0, 0)))
    rows_all = whole_rows.shape[1]
    pre_two = conv_forward(ext_low, w_bottom, rows_all, cols_low, depth_low)
    act_block = (
        jax.nn.silu(pre_two).astype(jnp.bfloat16).reshape(-1, rows_all, cols_low * depth_low)
    )
    act_two = lax.all_to_all(act_block, "gx", split_axis=1, concat_axis=0, tiled=True)
    cat_mid = jnp.concatenate([upsample(act_two, depth_low), act_one], axis=0)
    ext_mid = spatial_halo(cat_mid, depth_mid, 1)
    pre_three = conv_forward(ext_mid, w_middle, rows_mid, cols_mid, depth_mid)
    act_three = (
        jax.nn.silu(pre_three).astype(jnp.bfloat16).reshape(-1, rows_mid, cols_mid * depth_mid)
    )
    cat_top = jnp.concatenate([upsample(act_three, depth_mid), skip_input], axis=0)
    ext_top = spatial_halo(cat_top, Z, 2)
    pre_four = conv_forward(ext_top, w_upper, rows_fine, cols_fine, Z)
    features = (
        jax.nn.silu(pre_four).astype(jnp.bfloat16).reshape(top_chan, rows_fine, cols_fine * Z)
    )
    err_four = (cotangent.reshape(top_chan, -1).astype(jnp.float32) * silu_slope(pre_four)).astype(
        jnp.bfloat16
    )
    local_upper = weight_grad(ext_top, err_four, rows_fine, cols_fine, Z) * scale_fine
    dcat_top = conv_backward(
        spatial_halo(err_four.reshape(top_chan, rows_fine, cols_fine * Z), Z, 3),
        w_upper,
        rows_fine,
        cols_fine,
        Z,
    ).reshape(-1, rows_fine, cols_fine * Z)
    mid_chan = act_three.shape[0]
    err_three = (
        block_sum(dcat_top[:mid_chan], Z).reshape(mid_chan, -1) * silu_slope(pre_three)
    ).astype(jnp.bfloat16)
    local_middle = weight_grad(ext_mid, err_three, rows_mid, cols_mid, depth_mid) * scale_mid
    dcat_mid = conv_backward(
        spatial_halo(err_three.reshape(mid_chan, rows_mid, cols_mid * depth_mid), depth_mid, 4),
        w_middle,
        rows_mid,
        cols_mid,
        depth_mid,
    ).reshape(-1, rows_mid, cols_mid * depth_mid)
    low_chan = act_two.shape[0]
    dact_two = block_sum(dcat_mid[:low_chan], depth_mid)
    dact_block = lax.all_to_all(dact_two, "gx", split_axis=0, concat_axis=1, tiled=True)
    block_chan = dact_block.shape[0]
    err_two = (dact_block.reshape(block_chan, -1) * silu_slope(pre_two)).astype(jnp.bfloat16)
    part_bottom = weight_grad(ext_low, err_two, rows_all, cols_low, depth_low)
    err_grid = err_two.reshape(block_chan, rows_all, cols_low * depth_low)
    err_cols = extended_2(err_grid, (("gy", 2),), depth_low)
    err_ext = jnp.pad(err_cols, ((0, 0), (1, 1), (0, 0)))
    partial_sum = conv_backward(err_ext, w_bottom, rows_all, cols_low, depth_low).reshape(
        -1, rows_all, cols_low * depth_low
    )
    dpool_parts = lax.all_to_all(
        partial_sum.astype(jnp.bfloat16), "gx", split_axis=1, concat_axis=1, tiled=True
    ).astype(jnp.float32)
    dpool_mid = dpool_parts.reshape(
        dpool_parts.shape[0], lax.axis_size("gx"), rows_low, -1
    ).sum(axis=1)
    dact_one = dcat_mid[low_chan:] + upsample(dpool_mid, depth_low) / 8.0
    err_one = (dact_one.reshape(mid_chan, -1) * silu_slope(pre_one)).astype(jnp.bfloat16)
    local_encoder = weight_grad(ext_pool, err_one, rows_mid, cols_mid, depth_mid) * scale_mid
    (grad_encoder, grad_middle, grad_upper), grad_bottom = summed(
        (local_encoder, local_middle, local_upper), part_bottom * scale_low, 6
    )
    dpool_top = conv_backward(
        spatial_halo(err_one.reshape(mid_chan, rows_mid, cols_mid * depth_mid), depth_mid, 5),
        w_encoder,
        rows_mid,
        cols_mid,
        depth_mid,
    ).reshape(-1, rows_mid, cols_mid * depth_mid)
    grad_skip = (dcat_top[mid_chan:] + upsample(dpool_top, depth_mid) / 8.0).astype(jnp.bfloat16)
    return (features, grad_skip, grad_encoder, grad_bottom, grad_middle, grad_upper)


def solution(mesh):
    in_specs = (P(None, "gx", "gy"), P(), P("gx", None), P(), P(), P(None, "gx", "gy"))
    out_specs = (P(None, "gx", "gy"), P(None, "gx", "gy"), P(), P("gx", None), P(), P())
    return jax.shard_map(
        per_device, mesh=mesh, in_specs=in_specs, out_specs=out_specs, check_vma=False
    )
```

profile of v0, /device:TPU:3, one launch (start us, length us, event | category | flops | bytes accessed | tf_op | source)
XLA Modules:
  0.0 247.0 jit_solution(10914542008940713556)
XLA Ops:
  0.6 1.0 copy.231
  2.3 1.1 reshape.558
  8.4 7.2 %shard_map.109 = (bf16[32,128]{1,0:T(8,128)(2,1)}, bf16[32,128]{1,0:T(8,128)(2,1)}, bf16[32,128]{1,0:T(8,128)(2,1)}, bf16[32,128]{1,0:T(8,128)(2,1)}, bf16[32,12...) custom-call(bf16[32,128]{1,0:T(8,128)(2,1)} %pad.235.refs_0_, ...), custom_call_target="tpu_custom_call" | custom-call | tf_op jit(solution)/shard_map/pallas_call | solution.py:80
  20.3 3.4 %collective-permute-start = (bf16[64,1,4]{0,2,1:T(4,128)(2,1)S(1)}, bf16[64,1,4]{0,2,1:T(4,128)(2,1)S(1)}, u32[]{:S(2)}, u32[]{:S(2)}) collective-permute-start(bf16[64,1,4]{0,2,1:T(4,128)(2,1)S(1)} %get-tuple-element.204), channel_id=1, source_target_pairs={{0,1},{1,2},{2,3},{3,4},{4,5},{5,6},{6,7},{8,9},{9,10},{10,11},{11... | collective-permute-start | bytes 1544 | tf_op jit(solution)/shard_map/ppermute | solution.py:250
  23.6 1.9 collective-permute-start.1
  25.8 3.0 %collective-permute-done.1 = bf16[64,1,4]{0,2,1:T(4,128)(2,1)S(1)} collective-permute-done((bf16[64,1,4]{0,2,1:T(4,128)(2,1)S(1)}, bf16[64,1,4]{0,2,1:T(4,128)(2,1)S(1)}, u32[]{:S(2)}, u32[]{:S(2)}) %collective-permute-start.1) | collective-permute-done | bytes 544 | tf_op jit(solution)/shard_map/ppermute | solution.py:252
  28.9 6.5 %all_gather.3 = bf16[64,4,24]{0,2,1:T(8,128)(2,1)S(1)} all-gather(bf16[64,1,24]{0,2,1:T(8,128)(2,1)S(1)} %pad_maximum_fusion.4), channel_id=1, replica_groups=mesh['gx'=4,'gy'=8] {'gx'}, dimensions={1}, use_global_device_ids=true | all-gather | bytes 15360 | tf_op jit(solution)/shard_map/all_gather | solution.py:399
  36.9 3.4 %all-to-all-start = ((bf16[4,2,256]{2,1,0:T(2,128)(2,1)}), bf16[4,2,256]{2,1,0:T(2,128)(2,1)S(1)}, u32[]{:S(2)}, u32[]{:S(2)}) async-start(bf16[4,2,256]{2,1,0:T(2,128)(2,1)} %reshape.684), calls=%async_computation | async-start | bytes 8192 | tf_op jit(solution)/shard_map/all_to_all | solution.py:406
  41.1 1.0 reshape.653
  42.1 0.9 reshape.604
  42.9 1.0 reshape.624
  44.6 1.1 reshape.646
  46.8 0.9 rev.14
  47.7 1.0 copy.313
  50.4 2.1 rev.13
  52.5 1.7 copy.305
  55.0 1.7 reshape.648
  56.6 2.3 copy.307
  58.9 1.2 pad.283.w_ref
  66.1 9.8 %shard_map.112 = (bf16[192,128]{1,0:T(8,128)(2,1)}, bf16[192,128]{1,0:T(8,128)(2,1)}, bf16[192,128]{1,0:T(8,128)(2,1)}, bf16[192,128]{1,0:T(8,128)(2,1)}, bf16[1...) custom-call(bf16[192,128]{1,0:T(8,128)(2,1)} %pad.248.refs_0_, ...), custom_call_target="tpu_custom_call" | custom-call | tf_op jit(solution)/shard_map/pallas_call | solution.py:80
  76.8 0.9 copy.259
  77.6 0.9 copy.260
  78.5 0.8 slice_bitcast_fusion.16
  89.5 8.0 %shard_map.114 = (bf16[96,128]{1,0:T(8,128)(2,1)}, bf16[96,256]{1,0:T(8,128)(2,1)}, bf16[96,128]{1,0:T(8,128)(2,1)}, bf16[96,128]{1,0:T(8,128)(2,1)}, bf16[96,12...) custom-call(bf16[96,128]{1,0:T(8,128)(2,1)} %pad.258.refs_0_, ...), custom_call_target="tpu_custom_call" | custom-call | tf_op jit(solution)/shard_map/pallas_call | solution.py:80
  99.0 0.8 copy.274
  102.3 1.1 maximum_maximum_fusion
  103.8 1.5 shard_map.115
  110.9 7.0 %shard_map.116 = (bf16[32,128]{1,0:T(8,128)(2,1)}, bf16[32,256]{1,0:T(8,128)(2,1)}, bf16[32,128]{1,0:T(8,128)(2,1)}, bf16[32,128]{1,0:T(8,128)(2,1)}, bf16[32,12...) custom-call(bf16[32,128]{1,0:T(8,128)(2,1)} %pad.266.refs_0_, ...), custom_call_target="tpu_custom_call" | custom-call | tf_op jit(solution)/shard_map/pallas_call | solution.py:80
  122.5 0.9 maximum_maximum_fusion.2
  123.5 1.0 shard_map.117
  124.5 1.2 copy.339
  125.7 1.1 slice.624
  127.5 2.7 %shard_map.125 = f32[3,32,896]{2,1,0:T(8,128)S(1)} custom-call(bf16[96,2304]{1,0:T(8,128)(2,1)S(1)} %bitcast.332, bf16[32,1536]{1,0:T(8,128)(2,1)S(1)} %bitcast.336), custom_call_target="tpu_custom_call" | custom-call | tf_op jit(solution)/shard_map/pallas_call | solution.py:306
  135.8 6.8 %shard_map.118 = (bf16[64,128]{1,0:T(8,128)(2,1)}, bf16[64,128]{1,0:T(8,128)(2,1)}, bf16[64,128]{1,0:T(8,128)(2,1)}, bf16[64,128]{1,0:T(8,128)(2,1)}, bf16[64,12...) custom-call(bf16[64,128]{1,0:T(8,128)(2,1)} %pad.274.refs_0_, ...), custom_call_target="tpu_custom_call" | custom-call | tf_op jit(solution)/shard_map/pallas_call | solution.py:80
  152.1 3.5 %all-to-all-start.1 = ((f32[4,1,512]{2,1,0:T(1,128)}), f32[4,1,512]{2,1,0:T(1,128)S(1)}, u32[]{:S(2)}, u32[]{:S(2)}) async-start(f32[4,1,512]{2,1,0:T(1,128)} %reshape.686), calls=%async_computation.1 | async-start | bytes 16384 | tf_op jit(solution)/shard_map/all_to_all | solution.py:444
  155.5 1.2 shard_map.124
  156.7 0.9 slice_bitcast_fusion
  157.6 1.3 concatenate.140
  161.5 3.5 %collective-permute-start.2 = (bf16[32,4,4]{0,1,2:T(4,128)(2,1)S(1)}, bf16[32,4,4]{0,1,2:T(4,128)(2,1)S(1)}, u32[]{:S(2)}, u32[]{:S(2)}) collective-permute-start(bf16[32,4,4]{0,1,2:T(4,128)(2,1)S(1)} %get-tuple-element.196), channel_id=1, source_target_pairs={{0,1},{1,2},{2,3},{3,4},{4,5},{5,6},{6,7},{8,9},{9,10},{10,11},{11... | collective-permute-start | bytes 3080 | tf_op jit(solution)/shard_map/ppermute | solution.py:250
  165.0 1.9 collective-permute-start.3
  168.1 2.2 collective-permute-done.3
  171.7 4.9 %all-to-all-start.2 = ((bf16[4,2,512]{2,1,0:T(2,128)(2,1)}), bf16[4,2,512]{2,1,0:T(2,128)(2,1)S(1)}, u32[]{:S(2)}, u32[]{:S(2)}) async-start(bf16[4,2,512]{2,1,0:T(2,128)(2,1)} %reshape.688), calls=%async_computation.2 | async-start | bytes 16384 | tf_op jit(solution)/shard_map/all_to_all | solution.py:454
  176.6 3.1 %all-to-all-done.2 = bf16[4,2,512]{2,1,0:T(2,128)(2,1)S(1)} async-done(((bf16[4,2,512]{2,1,0:T(2,128)(2,1)}), bf16[4,2,512]{2,1,0:T(2,128)(2,1)S(1)}, u32[]{:S(2)}, u32[]{:S(2)}) %all-to-all-start.2) | async-done | bytes 8224 | tf_op jit(solution)/shard_map/all_to_all | solution.py:454
  180.9 0.9 concatenate.143.big
  181.7 38.3 %shard_map.127 = (bf16[64,7680]{1,0:T(8,128)(2,1)S(1)}, bf16[64,896]{1,0:T(8,128)(2,1)S(1)}) custom-call(bf16[64,7680]{1,0:T(8,128)(2,1)S(1)} %concatenate.143.big, bf16[64,896]{1,0:T(8,128)(2,1)S(1)} %fusion.4.low), custom_call_target="tpu_custom_call" | custom-call | tf_op jit(solution)/shard_map/pallas_call | solution.py:216
  220.9 1.3 slice_convert_fusion
  227.4 10.0 %shard_map.121 = (bf16[64,128]{1,0:T(8,128)(2,1)}, bf16[64,128]{1,0:T(8,128)(2,1)}, bf16[64,128]{1,0:T(8,128)(2,1)}, bf16[64,128]{1,0:T(8,128)(2,1)}, bf16[64,12...) custom-call(bf16[64,128]{1,0:T(8,128)(2,1)} %pad.287.refs_0_, ...), custom_call_target="tpu_custom_call" | custom-call | tf_op jit(solution)/shard_map/pallas_call | solution.py:80
  246.2 0.8 maximum_convert_fusion
  (325 shorter events, 84.6 us)
Async XLA Ops:
  2.0 23.6 %copy-start.9 = (bf16[32,1728]{1,0:T(8,128)(2,1)S(1)}, bf16[32,1728]{1,0:T(8,128)(2,1)}, u32[]{:S(2)}) copy-start(bf16[32,1728]{1,0:T(8,128)(2,1)} %param.8) | copy-start | bytes 331780
  19.6 20.7 %copy-start.13 = (bf16[32,4,256]{2,1,0:T(4,128)(2,1)S(1)}, bf16[32,4,256]{2,1,0:T(4,128)(2,1)}, u32[]{:S(2)}) copy-start(bf16[32,4,256]{2,1,0:T(4,128)(2,1)} %param.6) | copy-start | bytes 196612
  19.7 21.3 %copy-start.10 = (bf16[64,864]{1,0:T(8,128)(2,1)S(1)}, bf16[64,864]{1,0:T(8,128)(2,1)}, u32[]{:S(2)}) copy-start(bf16[64,864]{1,0:T(8,128)(2,1)} %param.7) | copy-start | bytes 331780
  20.1 5.7 %copy-start.7 = (f32[64,2,128]{2,1,0:T(2,128)}, f32[64,2,128]{2,1,0:T(2,128)S(1)}, u32[]{:S(2)}) copy-start(f32[64,2,128]{2,1,0:T(2,128)S(1)} %reshape.560) | copy-start | bytes 196612
  20.3 5.5 %collective-permute-start = (bf16[64,1,4]{0,2,1:T(4,128)(2,1)S(1)}, bf16[64,1,4]{0,2,1:T(4,128)(2,1)S(1)}, u32[]{:S(2)}, u32[]{:S(2)}) collective-permute-start(bf16[64,1,4]{0,2,1:T(4,128)(2,1)S(1)} %get-tuple-element.204), channel_id=1, source_target_pairs={{0,1},{1,2},{2,3},{3,4},{4,5},{5,6},{6,7},{8,9},{9,10},{10,11},{11... | collective-permute-start | bytes 1544 | tf_op jit(solution)/shard_map/ppermute | solution.py:250
  23.6 5.2 %collective-permute-start.1 = (bf16[64,1,4]{0,2,1:T(4,128)(2,1)S(1)}, bf16[64,1,4]{0,2,1:T(4,128)(2,1)S(1)}, u32[]{:S(2)}, u32[]{:S(2)}) collective-permute-start(bf16[64,1,4]{0,2,1:T(4,128)(2,1)S(1)} %get-tuple-element.205), channel_id=1, source_target_pairs={{1,0},{2,1},{3,2},{4,3},{5,4},{6,5},{7,6},{9,8},{10,9},{11,10},{12... | collective-permute-start | bytes 1544 | tf_op jit(solution)/shard_map/ppermute | solution.py:252
  25.7 16.3 %copy-start.6 = (bf16[32,2592]{1,0:T(8,128)(2,1)S(1)}, bf16[32,2592]{1,0:T(8,128)(2,1)}, u32[]{:S(2)}) copy-start(bf16[32,2592]{1,0:T(8,128)(2,1)} %param.10) | copy-start | bytes 497668
  35.4 8.5 %copy-start.1 = (bf16[64,5184]{1,0:T(8,128)(2,1)S(1)}, bf16[64,5184]{1,0:T(8,128)(2,1)}, u32[]{:S(2)}) copy-start(bf16[64,5184]{1,0:T(8,128)(2,1)} %param.9) | copy-start | bytes 1990660
  36.2 8.5 %copy-start.11 = (f32[32,4,16]{0,1,2:T(4,128)}, f32[32,4,16]{0,1,2:T(4,128)S(1)}, u32[]{:S(2)}) copy-start(f32[32,4,16]{0,1,2:T(4,128)S(1)} %copy.345) | copy-start | bytes 24580
  36.9 23.2 %all-to-all-start = ((bf16[4,2,256]{2,1,0:T(2,128)(2,1)}), bf16[4,2,256]{2,1,0:T(2,128)(2,1)S(1)}, u32[]{:S(2)}, u32[]{:S(2)}) async-start(bf16[4,2,256]{2,1,0:T(2,128)(2,1)} %reshape.684), calls=%async_computation | async-start | bytes 8192 | tf_op jit(solution)/shard_map/all_to_all | solution.py:406
  45.8 0.9 copy-start.5
  45.8 1.1 copy-start.4
  46.8 2.5 %copy-start.3 = (bf16[32,27,96]{2,1,0:T(8,128)(2,1)S(1)}, bf16[32,27,96]{2,1,0:T(8,128)(2,1)}, u32[]{:S(2)}) copy-start(bf16[32,27,96]{2,1,0:T(8,128)(2,1)} %reshape.624) | copy-start | bytes 497668
  83.2 1.4 copy-start.2
  103.7 1.7 copy-start.15
  152.1 8.3 %all-to-all-start.1 = ((f32[4,1,512]{2,1,0:T(1,128)}), f32[4,1,512]{2,1,0:T(1,128)S(1)}, u32[]{:S(2)}, u32[]{:S(2)}) async-start(f32[4,1,512]{2,1,0:T(1,128)} %reshape.686), calls=%async_computation.1 | async-start | bytes 16384 | tf_op jit(solution)/shard_map/all_to_all | solution.py:444
  158.9 0.8 copy-start.14
  158.9 2.4 copy-start.12
  161.5 6.6 %collective-permute-start.2 = (bf16[32,4,4]{0,1,2:T(4,128)(2,1)S(1)}, bf16[32,4,4]{0,1,2:T(4,128)(2,1)S(1)}, u32[]{:S(2)}, u32[]{:S(2)}) collective-permute-start(bf16[32,4,4]{0,1,2:T(4,128)(2,1)S(1)} %get-tuple-element.196), channel_id=1, source_target_pairs={{0,1},{1,2},{2,3},{3,4},{4,5},{5,6},{6,7},{8,9},{9,10},{10,11},{11... | collective-permute-start | bytes 3080 | tf_op jit(solution)/shard_map/ppermute | solution.py:250
  165.0 5.3 %collective-permute-start.3 = (bf16[32,4,4]{0,1,2:T(4,128)(2,1)S(1)}, bf16[32,4,4]{0,1,2:T(4,128)(2,1)S(1)}, u32[]{:S(2)}, u32[]{:S(2)}) collective-permute-start(bf16[32,4,4]{0,1,2:T(4,128)(2,1)S(1)} %get-tuple-element.197), channel_id=1, source_target_pairs={{1,0},{2,1},{3,2},{4,3},{5,4},{6,5},{7,6},{9,8},{10,9},{11,10},{12... | collective-permute-start | bytes 3080 | tf_op jit(solution)/shard_map/ppermute | solution.py:252
  167.8 12.1 %copy-start.8 = (f32[64,2,128]{2,1,0:T(2,128)S(1)}, f32[64,2,128]{2,1,0:T(2,128)}, u32[]{:S(2)}) copy-start(f32[64,2,128]{2,1,0:T(2,128)} %copy-done.7) | copy-start | bytes 196612
  171.7 8.0 %all-to-all-start.2 = ((bf16[4,2,512]{2,1,0:T(2,128)(2,1)}), bf16[4,2,512]{2,1,0:T(2,128)(2,1)S(1)}, u32[]{:S(2)}, u32[]{:S(2)}) async-start(bf16[4,2,512]{2,1,0:T(2,128)(2,1)} %reshape.688), calls=%async_computation.2 | async-start | bytes 16384 | tf_op jit(solution)/shard_map/all_to_all | solution.py:454
  222.2 22.3 %copy-start = (f32[96,1536]{0,1:T(8,128)S(1)}, f32[96,1536]{0,1:T(8,128)}, u32[]{:S(2)}) copy-start(f32[96,1536]{0,1:T(8,128)} %copy.339) | copy-start | bytes 1769476
where the time goes:
time: 250 us; the launch traced here: 247 us
  local copies, waits for them, and re-layouts  99 us (40%)
  Pallas kernels  97.6 us (39%)
  starting transfers between devices  22.5 us (9%)
  other arithmetic  10.9 us (4%)
  waiting for transfers between devices  8.34 us (3%)
  blocking collectives  6.51 us (3%)
    pallas_call x6, Pallas kernels, spatial_halo(): pl.pallas_call(functools.partial(halo_kernel, lax.axis_size('gx'), lax.ax...  48.7 us
    pallas_call x1, Pallas kernels, summed(): pl.pallas_call(functools.partial(sum_kernel, nx, ny, q, s), out_shape=[ja...  38.3 us
    pad x44, local copies, waits for them, and re-layouts, spatial_halo(): strips.append(jnp.pad(flat, ((0, 0), (0, -flat.shape[1] % 128))))  27 us
    reshape x41, local copies, waits for them, and re-layouts, spatial_halo(): strip[:, :shape[1] * shape[2]].reshape(shape)  22.7 us
    pallas_call x12, Pallas kernels, local_call(): pl.pallas_call(functools.partial(kernel, z_depth, row_count), out_shape=j...  10.6 us
    slice x12, local copies, waits for them, and re-layouts, spatial_halo(): strip[:, :shape[1] * shape[2]].reshape(shape)  9.64 us
    unnamed x68, local copies, waits for them, and re-layouts  8.23 us
    ppermute x2, starting transfers between devices, extended_2(): lax.ppermute(tail, axis, [(i, (i + 1) % count) for i in range(ends)])  6.89 us
  transfers between devices with their start and end apart: 7, of which 3 were waited for; matrix products, arithmetic and copies ran while one was open for 9% of the time, Pallas kernels for 1%

commit v1 on v0

--- a/solution.py
+++ b/solution.py
@@ -75,8 +75,7 @@
         if side[1] != 0:
             part = part[:, :, :width] if side[1] < 0 else part[:, :, length - width :]
         shapes.append(part.shape)
-        flat = part.reshape(channels, -1)
-        strips.append(jnp.pad(flat, ((0, 0), (0, -flat.shape[1] % 128))))
+        strips.append(part.reshape(channels, -1))
     landed = pl.pallas_call(
         functools.partial(halo_kernel, lax.axis_size("gx"), lax.axis_size("gy")),
         out_shape=[jax.ShapeDtypeStruct(strip.shape, strip.dtype) for strip in strips],
@@ -85,9 +84,7 @@
         scratch_shapes=[pltpu.SemaphoreType.DMA((8,)), pltpu.SemaphoreType.DMA((8,))],
         compiler_params=pltpu.CompilerParams(collective_id=number, has_side_effects=True),
     )(*strips)
-    parts = [
-        strip[:, : shape[1] * shape[2]].reshape(shape) for strip, shape in zip(landed, shapes)
-    ]
+    parts = [strip.reshape(shape) for strip, shape in zip(landed, shapes)]
     return jnp.concatenate(
         [
             jnp.concatenate(parts[0:3], axis=2),

time: 250 us -> 217 us (0.87)
  local copies, waits for them, and re-layouts: 99 us -> 62.1 us
  other arithmetic: 10.9 us -> 16.2 us
    pad x44 -> x0, local copies, waits for them, and re-layouts: 27 us -> none  [spatial_halo(): strips.append(jnp.pad(flat, ((0, 0), (0, -flat.shape[1] % 128))))]
    reshape x62 -> x33, local copies, waits for them, and re-layouts: 24.9 us -> 14.9 us  [the longest x21 13.6 us: spatial_halo(): strips.append(part.reshape(channels, -1))]
    pallas_call x0 -> x12, local copies, waits for them, and re-layouts: none -> 9.64 us  [spatial_halo(): pl.pallas_call(functools.partial(halo_kernel, lax.axis_size('gx'), lax.ax...]
    slice x12 -> x0, local copies, waits for them, and re-layouts: 9.64 us -> none  [spatial_halo(): strip[:, :shape[1] * shape[2]].reshape(shape)]
    concatenate x6, other arithmetic: 2.46 us -> 5.88 us  [spatial_halo(): jnp.concatenate([jnp.concatenate(parts[0:3], axis=2), jnp.concatenate([pa...]
  transfers between devices with their start and end apart: 7 -> 7, of which waited for: 3 -> 3; matrix products, arithmetic and copies ran while one was open for 9% -> 10% of each run, Pallas kernels for 1% -> 1%
where the time goes in v1:
time: 217 us; the launch traced here: 215 us
  Pallas kernels  97.6 us (45%)
  local copies, waits for them, and re-layouts  62.1 us (29%)
  starting transfers between devices  22.5 us (10%)
  other arithmetic  16.2 us (7%)
  waiting for transfers between devices  8.35 us (4%)
  blocking collectives  6.51 us (3%)
    pallas_call x6, Pallas kernels, spatial_halo(): pl.pallas_call(functools.partial(halo_kernel, lax.axis_size('gx'), lax.ax...  48.7 us
    pallas_call x1, Pallas kernels, summed(): pl.pallas_call(functools.partial(sum_kernel, nx, ny, q, s), out_shape=[ja...  38.3 us
    reshape x21, local copies, waits for them, and re-layouts, spatial_halo(): strips.append(part.reshape(channels, -1))  13.6 us
    pallas_call x12, Pallas kernels, local_call(): pl.pallas_call(functools.partial(kernel, z_depth, row_count), out_shape=j...  10.6 us
    pallas_call x12, local copies, waits for them, and re-layouts, spatial_halo(): pl.pallas_call(functools.partial(halo_kernel, lax.axis_size('gx'), lax.ax...  9.64 us
    unnamed x68, local copies, waits for them, and re-layouts  8.24 us
    ppermute x2, starting transfers between devices, extended_2(): lax.ppermute(tail, axis, [(i, (i + 1) % count) for i in range(ends)])  6.9 us
    all_gather x1, blocking collectives, per_device(): whole_rows = lax.all_gather(col_ext, 'gx', axis=1, tiled=True)  6.51 us
  transfers between devices with their start and end apart: 7, of which 3 were waited for; matrix products, arithmetic and copies ran while one was open for 10% of the time, Pallas kernels for 1%

profile of v1, /device:TPU:3, one launch (start us, length us, event | category | flops | bytes accessed | tf_op | source)
XLA Modules:
  0.0 215.3 jit_solution(2203664941607519069)
XLA Ops:
  0.6 1.0 copy.231
  3.5 1.1 reshape.558
  5.9 7.2 %shard_map.109 = (bf16[32,8]{1,0:T(8,128)(2,1)}, bf16[32,64]{1,0:T(8,128)(2,1)}, bf16[32,8]{1,0:T(8,128)(2,1)}, bf16[32,16]{1,0:T(8,128)(2,1)}, bf16[32,16]{1,0:...) custom-call(bf16[32,8]{1,0:T(8,128)(2,1)} %get-tuple-element.201.refs_0_, ...), custom_call_target="tpu_custom_call" | custom-call | tf_op jit(solution)/shard_map/pallas_call | solution.py:79
  14.9 0.9 maximum_maximum_fusion.5
  16.5 3.4 %collective-permute-start = (bf16[64,1,4]{0,2,1:T(4,128)(2,1)S(1)}, bf16[64,1,4]{0,2,1:T(4,128)(2,1)S(1)}, u32[]{:S(2)}, u32[]{:S(2)}) collective-permute-start(bf16[64,1,4]{0,2,1:T(4,128)(2,1)S(1)} %get-tuple-element.204), channel_id=1, source_target_pairs={{0,1},{1,2},{2,3},{3,4},{4,5},{5,6},{6,7},{8,9},{9,10},{10,11},{11... | collective-permute-start | bytes 1544 | tf_op jit(solution)/shard_map/ppermute | solution.py:247
  19.9 1.9 collective-permute-start.1
  22.0 3.0 %collective-permute-done.1 = bf16[64,1,4]{0,2,1:T(4,128)(2,1)S(1)} collective-permute-done((bf16[64,1,4]{0,2,1:T(4,128)(2,1)S(1)}, bf16[64,1,4]{0,2,1:T(4,128)(2,1)S(1)}, u32[]{:S(2)}, u32[]{:S(2)}) %collective-permute-start.1) | collective-permute-done | bytes 544 | tf_op jit(solution)/shard_map/ppermute | solution.py:249
  25.1 6.5 %all_gather.3 = bf16[64,4,24]{0,2,1:T(8,128)(2,1)S(1)} all-gather(bf16[64,1,24]{0,2,1:T(8,128)(2,1)S(1)} %pad_maximum_fusion.4), channel_id=1, replica_groups=mesh['gx'=4,'gy'=8] {'gx'}, dimensions={1}, use_global_device_ids=true | all-gather | bytes 15360 | tf_op jit(solution)/shard_map/all_gather | solution.py:396
  33.1 3.4 %all-to-all-start = ((bf16[4,2,256]{2,1,0:T(2,128)(2,1)}), bf16[4,2,256]{2,1,0:T(2,128)(2,1)S(1)}, u32[]{:S(2)}, u32[]{:S(2)}) async-start(bf16[4,2,256]{2,1,0:T(2,128)(2,1)} %reshape.684), calls=%async_computation | async-start | bytes 8192 | tf_op jit(solution)/shard_map/all_to_all | solution.py:403
  37.3 0.9 reshape.653
  38.3 0.9 reshape.604
  39.2 1.0 reshape.624
  40.8 1.1 reshape.646
  43.1 0.9 rev.14
  43.9 1.0 copy.313
  46.6 2.1 rev.13
  48.7 1.7 copy.305
  51.2 1.7 reshape.648
  52.8 2.3 %copy.307 = bf16[576,576]{1,0:T(8,128)(2,1)} copy(bf16[576,576]{0,1:T(8,128)(2,1)} %reshape.648) | data formatting | bytes 1327104 | tf_op jit(solution)/shard_map/reshape | solution.py:315
  55.1 1.2 pad.104.w_ref
  59.8 9.8 %shard_map.112 = (bf16[192,8]{1,0:T(8,128)(2,1)}, bf16[192,64]{1,0:T(8,128)(2,1)}, bf16[192,8]{1,0:T(8,128)(2,1)}, bf16[192,16]{1,0:T(8,128)(2,1)}, bf16[192,16]...) custom-call(bf16[192,8]{1,0:T(8,128)(2,1)} %get-tuple-element.165.refs_0_, ...), custom_call_target="tpu_custom_call" | custom-call | tf_op jit(solution)/shard_map/pallas_call | solution.py:79
  70.5 0.9 copy.260
  71.7 1.1 maximum_maximum_fusion.1
  77.3 7.9 %shard_map.114 = (bf16[96,16]{1,0:T(8,128)(2,1)}, bf16[96,256]{1,0:T(8,128)(2,1)}, bf16[96,16]{1,0:T(8,128)(2,1)}, bf16[96,64]{1,0:T(8,128)(2,1)}, bf16[96,64]{1...) custom-call(bf16[96,16]{1,0:T(8,128)(2,1)} %get-tuple-element.147.refs_0_, ...), custom_call_target="tpu_custom_call" | custom-call | tf_op jit(solution)/shard_map/pallas_call | solution.py:79
  87.2 1.1 maximum_maximum_fusion
  88.7 1.5 shard_map.115
  94.0 7.0 %shard_map.116 = (bf16[32,16]{1,0:T(8,128)(2,1)}, bf16[32,256]{1,0:T(8,128)(2,1)}, bf16[32,16]{1,0:T(8,128)(2,1)}, bf16[32,64]{1,0:T(8,128)(2,1)}, bf16[32,64]{1...) custom-call(bf16[32,16]{1,0:T(8,128)(2,1)} %get-tuple-element.173.refs_0_, ...), custom_call_target="tpu_custom_call" | custom-call | tf_op jit(solution)/shard_map/pallas_call | solution.py:79
  102.8 0.9 maximum_maximum_fusion.2
  103.9 1.0 shard_map.117
  104.8 1.2 copy.339
  106.0 1.1 slice.448
  109.1 2.7 %shard_map.125 = f32[3,32,896]{2,1,0:T(8,128)S(1)} custom-call(bf16[96,2304]{1,0:T(8,128)(2,1)S(1)} %bitcast.288, bf16[32,1536]{1,0:T(8,128)(2,1)S(1)} %bitcast.292), custom_call_target="tpu_custom_call" | custom-call | tf_op jit(solution)/shard_map/pallas_call | solution.py:303
  113.7 6.8 %shard_map.118 = (bf16[64,8]{1,0:T(8,128)(2,1)}, bf16[64,64]{1,0:T(8,128)(2,1)}, bf16[64,8]{1,0:T(8,128)(2,1)}, bf16[64,16]{1,0:T(8,128)(2,1)}, bf16[64,16]{1,0:...) custom-call(bf16[64,8]{1,0:T(8,128)(2,1)} %get-tuple-element.189.refs_0_, ...), custom_call_target="tpu_custom_call" | custom-call | tf_op jit(solution)/shard_map/pallas_call | solution.py:79
  122.2 0.9 maximum_maximum_fusion.3
  126.4 3.5 %all-to-all-start.1 = ((f32[4,1,512]{2,1,0:T(1,128)}), f32[4,1,512]{2,1,0:T(1,128)S(1)}, u32[]{:S(2)}, u32[]{:S(2)}) async-start(f32[4,1,512]{2,1,0:T(1,128)} %reshape.686), calls=%async_computation.1 | async-start | bytes 16384 | tf_op jit(solution)/shard_map/all_to_all | solution.py:441
  129.9 1.2 shard_map.124
  131.0 0.9 slice_bitcast_fusion
  131.9 1.3 concatenate.140
  135.8 3.5 %collective-permute-start.2 = (bf16[32,4,4]{0,1,2:T(4,128)(2,1)S(1)}, bf16[32,4,4]{0,1,2:T(4,128)(2,1)S(1)}, u32[]{:S(2)}, u32[]{:S(2)}) collective-permute-start(bf16[32,4,4]{0,1,2:T(4,128)(2,1)S(1)} %get-tuple-element.196), channel_id=1, source_target_pairs={{0,1},{1,2},{2,3},{3,4},{4,5},{5,6},{6,7},{8,9},{9,10},{10,11},{11... | collective-permute-start | bytes 3080 | tf_op jit(solution)/shard_map/ppermute | solution.py:247
  139.4 1.9 collective-permute-start.3
  142.4 2.2 %collective-permute-done.3 = bf16[32,4,4]{0,1,2:T(4,128)(2,1)S(1)} collective-permute-done((bf16[32,4,4]{0,1,2:T(4,128)(2,1)S(1)}, bf16[32,4,4]{0,1,2:T(4,128)(2,1)S(1)}, u32[]{:S(2)}, u32[]{:S(2)}) %collective-permute-start.3) | collective-permute-done | bytes 1056 | tf_op jit(solution)/shard_map/ppermute | solution.py:249
  146.1 4.9 %all-to-all-start.2 = ((bf16[4,2,512]{2,1,0:T(2,128)(2,1)}), bf16[4,2,512]{2,1,0:T(2,128)(2,1)S(1)}, u32[]{:S(2)}, u32[]{:S(2)}) async-start(bf16[4,2,512]{2,1,0:T(2,128)(2,1)} %reshape.688), calls=%async_computation.2 | async-start | bytes 16384 | tf_op jit(solution)/shard_map/all_to_all | solution.py:451
  151.0 3.1 %all-to-all-done.2 = bf16[4,2,512]{2,1,0:T(2,128)(2,1)S(1)} async-done(((bf16[4,2,512]{2,1,0:T(2,128)(2,1)}), bf16[4,2,512]{2,1,0:T(2,128)(2,1)S(1)}, u32[]{:S(2)}, u32[]{:S(2)}) %all-to-all-start.2) | async-done | bytes 8224 | tf_op jit(solution)/shard_map/all_to_all | solution.py:451
  156.4 0.9 concatenate.143.big
  157.2 38.3 %shard_map.127 = (bf16[64,7680]{1,0:T(8,128)(2,1)S(1)}, bf16[64,896]{1,0:T(8,128)(2,1)S(1)}) custom-call(bf16[64,7680]{1,0:T(8,128)(2,1)S(1)} %concatenate.143.big, bf16[64,896]{1,0:T(8,128)(2,1)S(1)} %fusion.4.low), custom_call_target="tpu_custom_call" | custom-call | tf_op jit(solution)/shard_map/pallas_call | solution.py:213
  196.4 1.3 slice_convert_fusion
  199.2 9.9 %shard_map.121 = (bf16[64,8]{1,0:T(8,128)(2,1)}, bf16[64,64]{1,0:T(8,128)(2,1)}, bf16[64,8]{1,0:T(8,128)(2,1)}, bf16[64,16]{1,0:T(8,128)(2,1)}, bf16[64,16]{1,0:...) custom-call(bf16[64,8]{1,0:T(8,128)(2,1)} %get-tuple-element.181.refs_0_, ...), custom_call_target="tpu_custom_call" | custom-call | tf_op jit(solution)/shard_map/pallas_call | solution.py:79
  211.0 0.9 maximum_maximum_fusion.4
  (252 shorter events, 52.4 us)
Async XLA Ops:
  1.7 20.2 %copy-start.9 = (bf16[32,1728]{1,0:T(8,128)(2,1)S(1)}, bf16[32,1728]{1,0:T(8,128)(2,1)}, u32[]{:S(2)}) copy-start(bf16[32,1728]{1,0:T(8,128)(2,1)} %param.8) | copy-start | bytes 331780
  15.8 20.7 %copy-start.13 = (bf16[32,4,256]{2,1,0:T(4,128)(2,1)S(1)}, bf16[32,4,256]{2,1,0:T(4,128)(2,1)}, u32[]{:S(2)}) copy-start(bf16[32,4,256]{2,1,0:T(4,128)(2,1)} %param.6) | copy-start | bytes 196612
  15.9 21.3 %copy-start.10 = (bf16[64,864]{1,0:T(8,128)(2,1)S(1)}, bf16[64,864]{1,0:T(8,128)(2,1)}, u32[]{:S(2)}) copy-start(bf16[64,864]{1,0:T(8,128)(2,1)} %param.7) | copy-start | bytes 331780
  16.3 21.0 %copy-start.7 = (f32[64,2,128]{2,1,0:T(2,128)}, f32[64,2,128]{2,1,0:T(2,128)S(1)}, u32[]{:S(2)}) copy-start(f32[64,2,128]{2,1,0:T(2,128)S(1)} %reshape.560) | copy-start | bytes 196612
  16.5 5.5 %collective-permute-start = (bf16[64,1,4]{0,2,1:T(4,128)(2,1)S(1)}, bf16[64,1,4]{0,2,1:T(4,128)(2,1)S(1)}, u32[]{:S(2)}, u32[]{:S(2)}) collective-permute-start(bf16[64,1,4]{0,2,1:T(4,128)(2,1)S(1)} %get-tuple-element.204), channel_id=1, source_target_pairs={{0,1},{1,2},{2,3},{3,4},{4,5},{5,6},{6,7},{8,9},{9,10},{10,11},{11... | collective-permute-start | bytes 1544 | tf_op jit(solution)/shard_map/ppermute | solution.py:247
  19.9 5.2 %collective-permute-start.1 = (bf16[64,1,4]{0,2,1:T(4,128)(2,1)S(1)}, bf16[64,1,4]{0,2,1:T(4,128)(2,1)S(1)}, u32[]{:S(2)}, u32[]{:S(2)}) collective-permute-start(bf16[64,1,4]{0,2,1:T(4,128)(2,1)S(1)} %get-tuple-element.205), channel_id=1, source_target_pairs={{1,0},{2,1},{3,2},{4,3},{5,4},{6,5},{7,6},{9,8},{10,9},{11,10},{12... | collective-permute-start | bytes 1544 | tf_op jit(solution)/shard_map/ppermute | solution.py:249
  22.0 16.3 %copy-start.6 = (bf16[32,2592]{1,0:T(8,128)(2,1)S(1)}, bf16[32,2592]{1,0:T(8,128)(2,1)}, u32[]{:S(2)}) copy-start(bf16[32,2592]{1,0:T(8,128)(2,1)} %param.10) | copy-start | bytes 497668
  31.6 8.6 %copy-start.1 = (bf16[64,5184]{1,0:T(8,128)(2,1)S(1)}, bf16[64,5184]{1,0:T(8,128)(2,1)}, u32[]{:S(2)}) copy-start(bf16[64,5184]{1,0:T(8,128)(2,1)} %param.9) | copy-start | bytes 1990660
  32.4 7.8 %copy-start.11 = (f32[32,4,16]{0,1,2:T(4,128)}, f32[32,4,16]{0,1,2:T(4,128)S(1)}, u32[]{:S(2)}) copy-start(f32[32,4,16]{0,1,2:T(4,128)S(1)} %copy.345) | copy-start | bytes 24580
  33.1 23.2 %all-to-all-start = ((bf16[4,2,256]{2,1,0:T(2,128)(2,1)}), bf16[4,2,256]{2,1,0:T(2,128)(2,1)S(1)}, u32[]{:S(2)}, u32[]{:S(2)}) async-start(bf16[4,2,256]{2,1,0:T(2,128)(2,1)} %reshape.684), calls=%async_computation | async-start | bytes 8192 | tf_op jit(solution)/shard_map/all_to_all | solution.py:403
  42.0 0.9 copy-start.5
  42.0 1.1 copy-start.4
  43.1 2.5 %copy-start.3 = (bf16[32,27,96]{2,1,0:T(8,128)(2,1)S(1)}, bf16[32,27,96]{2,1,0:T(8,128)(2,1)}, u32[]{:S(2)}) copy-start(bf16[32,27,96]{2,1,0:T(8,128)(2,1)} %reshape.624) | copy-start | bytes 497668
  72.9 1.4 copy-start.2
  88.6 1.7 copy-start.15
  126.4 8.3 %all-to-all-start.1 = ((f32[4,1,512]{2,1,0:T(1,128)}), f32[4,1,512]{2,1,0:T(1,128)S(1)}, u32[]{:S(2)}, u32[]{:S(2)}) async-start(f32[4,1,512]{2,1,0:T(1,128)} %reshape.686), calls=%async_computation.1 | async-start | bytes 16384 | tf_op jit(solution)/shard_map/all_to_all | solution.py:441
  133.2 0.8 copy-start.14
  133.2 2.4 %copy-start.12 = (f32[32,4,16]{0,1,2:T(4,128)S(1)}, f32[32,4,16]{0,1,2:T(4,128)}, u32[]{:S(2)}) copy-start(f32[32,4,16]{0,1,2:T(4,128)} %copy-done.11) | copy-start | bytes 24580
  135.8 6.6 %collective-permute-start.2 = (bf16[32,4,4]{0,1,2:T(4,128)(2,1)S(1)}, bf16[32,4,4]{0,1,2:T(4,128)(2,1)S(1)}, u32[]{:S(2)}, u32[]{:S(2)}) collective-permute-start(bf16[32,4,4]{0,1,2:T(4,128)(2,1)S(1)} %get-tuple-element.196), channel_id=1, source_target_pairs={{0,1},{1,2},{2,3},{3,4},{4,5},{5,6},{6,7},{8,9},{9,10},{10,11},{11... | collective-permute-start | bytes 3080 | tf_op jit(solution)/shard_map/ppermute | solution.py:247
  139.4 5.3 %collective-permute-start.3 = (bf16[32,4,4]{0,1,2:T(4,128)(2,1)S(1)}, bf16[32,4,4]{0,1,2:T(4,128)(2,1)S(1)}, u32[]{:S(2)}, u32[]{:S(2)}) collective-permute-start(bf16[32,4,4]{0,1,2:T(4,128)(2,1)S(1)} %get-tuple-element.197), channel_id=1, source_target_pairs={{1,0},{2,1},{3,2},{4,3},{5,4},{6,5},{7,6},{9,8},{10,9},{11,10},{12... | collective-permute-start | bytes 3080 | tf_op jit(solution)/shard_map/ppermute | solution.py:249
  142.2 12.1 %copy-start.8 = (f32[64,2,128]{2,1,0:T(2,128)S(1)}, f32[64,2,128]{2,1,0:T(2,128)}, u32[]{:S(2)}) copy-start(f32[64,2,128]{2,1,0:T(2,128)} %copy-done.7) | copy-start | bytes 196612
  146.1 8.0 %all-to-all-start.2 = ((bf16[4,2,512]{2,1,0:T(2,128)(2,1)}), bf16[4,2,512]{2,1,0:T(2,128)(2,1)S(1)}, u32[]{:S(2)}, u32[]{:S(2)}) async-start(bf16[4,2,512]{2,1,0:T(2,128)(2,1)} %reshape.688), calls=%async_computation.2 | async-start | bytes 16384 | tf_op jit(solution)/shard_map/all_to_all | solution.py:451
  197.7 15.0 %copy-start = (f32[96,1536]{0,1:T(8,128)S(1)}, f32[96,1536]{0,1:T(8,128)}, u32[]{:S(2)}) copy-start(f32[96,1536]{0,1:T(8,128)} %copy.339) | copy-start | bytes 1769476
